TPU v7x, 512 devices: a whole 4x4x16 slice. The times are simulated.
512 devices in a mesh: section: 16 (over z), dp: 32 (over y, x, core).
Axes of the slice: x: 4, y: 4, z: 16, core: 2. Of those that a mesh axis runs over, the one named last changes fastest.
Arguments:
- acts: bfloat16 [16, 16384, 2048], P('section', 'dp'), may hold values from -24 to 24
- key_grads: bfloat16 [16, 16384, 512], P('section', 'dp'), may hold values from -0.013531647 to 0.013531647
- key_weight: bfloat16 [16, 2048, 512], P('section', 'dp'), may hold values from -0.25 to 0.25
- lengths: int32 [32, 16], P('dp'), may hold values from 1 to 128, as said below
- threshold: float32 [], replicated, may hold values from 8 to 24
Outputs:
- act_grad: bfloat16 [16, 16384, 2048], P('section', 'dp')
- weight_grad: float32 [16, 2048, 512], P('section', 'dp')
Inputs may be any that keep to these rules, and one draw needn't show every extreme that they name: `lengths`: each row sums to 512, and its longest patient has exactly 128 tokens.
All inputs are finite; a program needn't handle non-finite values.
Results may differ from a plain program's by a relative error of at most 0.002.
Values may be sent and summed in bfloat16 or wider, within the bound.
A program may use at most 64 MiB of HBM per device.

v0:
```python
import jax
import jax.numpy as jnp
from jax import lax
from jax.sharding import PartitionSpec as P


def segment_of(lengths_row, count):
    ends = jnp.cumsum(lengths_row)
    position = jnp.arange(count, dtype=jnp.int32)
    return jnp.sum((position[:, None] >= ends[None, :]).astype(jnp.int32), axis=1)


def per_patient(rows_seg, rowsum, patients):
    patient = jnp.arange(patients, dtype=jnp.int32)
    onehot = rows_seg[..., None] == patient
    return jnp.sum(
        jnp.where(onehot, rowsum[..., None], jnp.float32(0.0)), axis=tuple(range(rowsum.ndim))
    )


def masked_norms(inputs, grads, seg, patients):
    tokens_here = inputs.shape[0]
    block = min(512, tokens_here)
    count = tokens_here // block
    contract = (((1,), (1,)), ((), ()))

    def one_block(index):
        gram_x = lax.dot_general(inputs, inputs, contract, preferred_element_type=jnp.float32)
        gram_g = lax.dot_general(grads, grads, contract, preferred_element_type=jnp.float32)
        same = seg[:, None] == seg[None, :]
        rowsum = jnp.sum(jnp.where(same, gram_x * gram_g, jnp.float32(0.0)), axis=1)
        return per_patient(seg, rowsum, patients)

    return jnp.sum(lax.map(one_block, jnp.arange(count)), axis=0)


def shards(acts, key_grads, key_weight, lengths, threshold):
    inputs = acts[0]
    grads = key_grads[0]
    patients = lengths.shape[1]
    seg = segment_of(lengths[0], inputs.shape[0])
    squares = masked_norms(inputs, grads, seg, patients)
    total = lax.psum(squares, "section")
    norm = jnp.sqrt(total)
    factor = threshold / jnp.maximum(norm, threshold)
    patient = jnp.arange(patients, dtype=jnp.int32)
    token_factor = jnp.sum(
        jnp.where(seg[:, None] == patient[None, :], factor[None, :], jnp.float32(0.0)), axis=1
    )
    scaled = (grads.astype(jnp.float32) * token_factor[:, None]).astype(jnp.bfloat16)
    act_part = lax.dot_general(
        grads,
        lax.all_gather(key_weight[0], "dp", axis=0, tiled=True),
        (((1,), (1,)), ((), ())),
        preferred_element_type=jnp.float32,
    ).astype(jnp.bfloat16)
    weight_part = lax.psum_scatter(
        lax.dot_general(
            inputs, scaled, (((0,), (0,)), ((), ())), preferred_element_type=jnp.float32
        ),
        "dp",
        scatter_dimension=0,
        tiled=True,
    )
    return (act_part[None], weight_part[None])


def solution(mesh):
    in_specs = (
        P("section", "dp", None),
        P("section", "dp", None),
        P("section", "dp", None),
        P("dp", None),
        P(),
    )
    out_specs = (P("section", "dp", None), P("section", "dp", None))
    return jax.shard_map(shards, mesh=mesh, in_specs=in_specs, out_specs=out_specs, check_vma=False)
```

profile of v0, /device:TPU:1, one launch (start us, length us, event | category | flops | bytes accessed | tf_op | source)
XLA Modules:
  0.0 191.6 jit_solution(15798087647202264948)
XLA Ops:
  7.2 0.0 copy-start
  7.2 0.0 all-gather.3.cloned.1.call-start
  7.2 0.7 all-gather.3.cloned.1.call-update
  7.9 0.0 reduce-scatter.4.cloned.1.call-start
  8.0 0.7 copy.13
  8.7 0.1 reduce
  9.5 0.1 convert_reduce_fusion
  9.6 1.7 fusion.16
  11.3 0.0 copy-done
  11.3 0.0 copy-start.1
  11.3 1.3 fusion.11
  12.6 0.1 select_reduce_fusion.1
  12.7 31.2 %psum.7 = f32[16]{0:T(128)S(1)} all-reduce(f32[16]{0:T(128)S(1)} %select_reduce_fusion.1), channel_id=1, replica_groups=mesh['section'=16,'dp'=32] {'section'}, use_global_device_ids=true, to_apply=%region_4.5 | all-reduce | flops 16 | bytes 128 | tf_op jit(solution)/shard_map/psum | solution.py:43
  44.0 0.1 select_reduce_fusion
  44.1 0.0 copy-done.1
  44.1 3.4 %convolution_bitcast_fusion = f32[2048,512]{0,1:T(8,128)} fusion(bf16[1,512,2048]{2,1,0:T(8,128)(2,1)S(1)} %copy-done, bf16[1,512,512]{2,1,0:T(8,128)(2,1)S(1)} %copy-done.1, f32[512]{0:T(512)S(1)} %select_reduce_fusion), kind=kOutput, calls=%fused_computation | convolution fusion | flops 1074528256 | bytes 6817792 | tf_op jit(solution)/shard_map/dot_general | solution.py:58
  47.4 5.3 %copy.15 = f32[2048,512]{1,0:T(8,128)} copy(f32[2048,512]{0,1:T(8,128)} %convolution_bitcast_fusion) | data formatting | bytes 8388608
  52.8 0.0 reduce-scatter.4.cloned.1.call-update
  52.8 23.3 %all-gather.3.cloned.1.call-done = bf16[1,2048,512]{2,1,0:T(8,128)(2,1)} async-done(((bf16[1,64,512]{2,1,0:T(8,128)(2,1)}), bf16[1,2048,512]{2,1,0:T(8,128)(2,1)}) %all-gather.3.cloned.1.call-update) | async-done | bytes 2097168 | tf_op jit(solution)/shard_map/all_gather | solution.py:53
  76.1 4.2 %fusion = bf16[1,512,2048]{2,1,0:T(8,128)(2,1)} fusion(bf16[1,2048,512]{2,1,0:T(8,128)(2,1)} %all-gather.3.cloned.1.call-done, bf16[1,512,512]{2,1,0:T(8,128)(2,1)S(1)} %copy-done.1), kind=kOutput, calls=%fused_computation.2 | convolution fusion | flops 1074790400 | bytes 4718592 | tf_op jit(solution)/shard_map/dot_general | solution.py:51
  80.3 102.7 %reduce-scatter.4.cloned.1.call-done = f32[64,512]{1,0:T(8,128)} async-done(((f32[2048,512]{1,0:T(8,128)}), f32[64,512]{1,0:T(8,128)}) %reduce-scatter.4.cloned.1.call-update) | async-done | bytes 131088
  183.0 1.0 copy.16
  184.0 0.8 copy.14
  (2 shorter events, 0.0 us)
Async XLA Ops:
  7.2 4.1 %copy-start = (bf16[1,512,2048]{2,1,0:T(8,128)(2,1)S(1)}, bf16[1,512,2048]{2,1,0:T(8,128)(2,1)}, u32[]{:S(2)}) copy-start(bf16[1,512,2048]{2,1,0:T(8,128)(2,1)} %param.5) | copy-start | bytes 6291460
  7.2 68.9 %all-gather.3.cloned.1.call-start = ((), (), s32[]{:S(2)}) async-start(), calls=%async_computation.1 | async-start | bytes 2162688 | tf_op jit(solution)/shard_map/all_gather | solution.py:53
  7.9 175.1 %reduce-scatter.4.cloned.1.call-start = ((), (), s32[]{:S(2)}) async-start(), calls=%async_computation.2 | async-start | bytes 4325376
  11.3 32.8 %copy-start.1 = (bf16[1,512,512]{2,1,0:T(8,128)(2,1)S(1)}, bf16[1,512,512]{2,1,0:T(8,128)(2,1)}, u32[]{:S(2)}) copy-start(bf16[1,512,512]{2,1,0:T(8,128)(2,1)} %param.6) | copy-start | bytes 1572868
Sparse Core Ops, SparseCore 0:
  11.1 64.9 all-gather.2
  80.6 102.3 reduce-scatter.3
where the time goes:
time: 192 us
  waiting for transfers between devices  127 us (66%)
  blocking collectives  31.2 us (16%)
  between operations  14.7 us (8%)
  matrix products  10.5 us (5%)
  local copies, waits for them, and re-layouts  7.9 us (4%)
    unnamed x3, waiting for transfers between devices  103 us
    psum x1, blocking collectives, shards(): total = lax.psum(squares, 'section')  31.2 us
    all_gather x1, waiting for transfers between devices, shards(): lax.all_gather(key_weight[0], 'dp', axis=0, tiled=True)  23.3 us
    unnamed x7, local copies, waits for them, and re-layouts  7.17 us
    dot_general x1, matrix products, shards(): lax.dot_general(grads, lax.all_gather(key_weight[0], 'dp', axis=0, tiled=...  4.19 us
  transfers between devices with their start and end apart: 2, of which 2 were waited for; matrix products, arithmetic and copies ran while one was open for 9% of the time, Pallas kernels for 0%

commit v1 on v0

v1 whole, which is shorter than its diff:
```python
import jax
import jax.numpy as jnp
from jax import lax
from jax.experimental import pallas as pl
from jax.experimental.pallas import tpu as pltpu
from jax.sharding import PartitionSpec as P

MESH = pl.DeviceIdType.MESH
F32, BF16 = jnp.float32, jnp.bfloat16
NT = (((1,), (1,)), ((), ()))
D, KV, TOK, PAT = 2048, 512, 512, 16
POS = {2: 0, 1: 1, 3: 2, 0: 3}
GROUPS = ((0, 1), (1, 3), (3, 4))
N_SEMS = 108


def kernel(
    acts_hbm, kg_hbm, w_hbm, len_ref, thr_ref, act_out, wg_out,
    acts, kg, kgs, kgt, sct, wr, act_v,
    zv, zr, z2s, z2r, z9s, z9r,
    pb, pc, pf, ra, cb, rx, ss, ra2, cb2, rx2, tb, wsw,
    ssem, rsem, lsem,
):
    z = lax.axis_index("section")
    dp = lax.axis_index("dp")
    core = lax.rem(dp, 2)
    xx = lax.rem(lax.div(dp, 2), 4)
    yy = lax.div(dp, 8)

    def dev(dy=0, dx=0, dc=0, dz=0):
        y2, x2 = lax.rem(yy + dy + 4, 4), lax.rem(xx + dx + 4, 4)
        c2 = 1 - core if dc else core
        return (lax.rem(z + dz + 16, 16), (y2 * 4 + x2) * 2 + c2)

    started = []

    def send(src, dst, to):
        k = len(started)
        copy = pltpu.make_async_remote_copy(
            src_ref=src, dst_ref=dst, send_sem=ssem.at[k], recv_sem=rsem.at[k],
            device_id=to, device_id_type=MESH,
        )
        copy.start()
        started.append(copy)
        return copy

    load_kg = pltpu.make_async_copy(kg_hbm, kg, lsem.at[0])
    load_acts = pltpu.make_async_copy(acts_hbm, acts.at[0], lsem.at[1])
    load_w = pltpu.make_async_copy(w_hbm, wr.at[0, 0, core], lsem.at[2])
    load_kg.start()
    load_acts.start()
    load_w.start()

    near = [dev(dc=1), dev(dx=1), dev(dx=-1), dev(dy=1), dev(dy=-1)]
    zs = [1, -1, 2, -2, 3, -3, 4, -4]
    partners = near + [dev(dz=k) for k in zs] + [dev(dz=4, dc=1), dev(dz=-4, dc=1)]
    barrier = pltpu.get_barrier_semaphore()
    for who in partners:
        pl.semaphore_signal(barrier, inc=1, device_id=who, device_id_type=MESH)

    lane = lax.broadcasted_iota(jnp.int32, (1, TOK), 1)
    sub = lax.broadcasted_iota(jnp.int32, (TOK, 1), 0)
    seg_row = jnp.zeros((1, TOK), jnp.int32)
    seg_col = jnp.zeros((TOK, 1), jnp.int32)
    end = jnp.int32(0)
    for p in range(PAT):
        end = end + len_ref[0, p]
        seg_row = seg_row + (lane >= end).astype(jnp.int32)
        seg_col = seg_col + (sub >= end).astype(jnp.int32)

    load_kg.wait()
    load_acts.wait()

    def masked(rows, cols):
        (r0, r1), (c0, c1) = rows, cols
        gx = lax.dot_general(acts[0, r0:r1], acts[0, c0:c1], NT, preferred_element_type=F32)
        gg = lax.dot_general(kg[r0:r1], kg[c0:c1], NT, preferred_element_type=F32)
        same = seg_col[r0:r1] == seg_row[:, c0:c1]
        return same, jnp.sum(jnp.where(same, gx * gg, 0.0), axis=1, keepdims=True)

    def spread(same, r):
        return jnp.sum(jnp.where(same, r, 0.0), axis=0, keepdims=True)

    same_a, r_a = masked((0, 256), (0, 256))
    same_c, r_c = masked((128, 256), (256, 384))
    same_b, r_b = masked((256, 512), (256, 512))
    r_1 = r_a[128:] + 2.0 * r_c
    same_t = seg_col[256:384] == seg_row[:, 128:256]
    v_a = spread(same_a[:128], r_a[:128]) + spread(same_a[128:], r_1)
    v_b = spread(same_b, r_b)
    zv[:, 0:128] = v_a[:, 0:128]
    zv[:, 128:256] = v_a[:, 128:256] + spread(same_t, r_b[:128])
    zv[:, 256:384] = v_b[:, 0:128] + spread(same_c, r_1)
    zv[:, 384:512] = v_b[:, 128:256]

    pl.semaphore_wait(barrier, len(partners))

    z1 = [send(zv, zr.at[i], dev(dz=k)) for i, k in enumerate(zs)]

    load_w.wait()
    step = (lambda s: dev(dx=s), lambda s: dev(dy=s))

    def at(h, d1, d2):
        return (d2, d1) if h == 0 else (d1, d2)

    def slot(h, d1, d2, lo=0, hi=32):
        return wr.at[(*at(h, d1, d2), core, pl.ds(32 * h + lo, hi - lo))]

    g_a1, g_a2, g_b1, g_b2 = {}, {}, {}, {}
    for h in range(2):
        g_a1[h] = (
            send(slot(h, 0, 0), slot(h, 3, 0), step[h](1)),
            send(slot(h, 0, 0), slot(h, 1, 0), step[h](-1)),
        )
    share_kg = send(
        kg.at[:, pl.ds(pl.multiple_of(256 * (1 - core), 256), 256)], kgs, dev(dc=1)
    )
    share_acts = send(acts.at[0], acts.at[1], dev(dc=1))

    def second(h, d1):
        return (
            send(slot(h, d1, 0), slot(h, d1, 3), step[1 - h](1)),
            send(slot(h, d1, 0), slot(h, d1, 1), step[1 - h](-1)),
        )

    def second_forward(h, d1):
        for c in g_b1[h, d1]:
            c.wait_recv()
        g_b2[h, d1] = (
            send(slot(h, d1, 3, 0, 16), slot(h, d1, 2, 0, 16), step[1 - h](1)),
            send(slot(h, d1, 1, 16, 32), slot(h, d1, 2, 16, 32), step[1 - h](-1)),
        )

    for h in range(2):
        g_b1[h, 0] = second(h, 0)

    own = pl.multiple_of(256 * core, 256)
    kgt[:, 0:512] = kg[:, pl.ds(own, 256)].T

    for h in range(2):
        for c in g_a1[h]:
            c.wait_recv()
        g_a2[h] = (
            send(slot(h, 3, 0, 0, 16), slot(h, 2, 0, 0, 16), step[h](1)),
            send(slot(h, 1, 0, 16, 32), slot(h, 2, 0, 16, 32), step[h](-1)),
        )
    for h in range(2):
        for d1 in (1, 3):
            g_b1[h, d1] = second(h, d1)
    for h in range(2):
        for c in g_a2[h]:
            c.wait_recv()
        g_b1[h, 2] = second(h, 2)
        second_forward(h, 0)

    share_kg.wait_recv()
    kgt[:, 512:1024] = kgs[...].T

    for c in z1:
        c.wait_recv()
    up = zr[0] + zr[2] + zr[4]
    down = zr[1] + zr[3] + zr[5]
    z2s[0] = up + zr[6]
    z2s[1] = down
    nine = zv[...] + (up + down) + (zr[6] + zr[7])
    z9s[...] = nine
    z2 = [
        send(z2s.at[0], z2r.at[0, 0], dev(dz=4)),
        send(z2s.at[1], z2r.at[0, 1], dev(dz=-4)),
        send(z2s.at[0], z2r.at[1, 0], dev(dz=4, dc=1)),
        send(z2s.at[1], z2r.at[1, 1], dev(dz=-4, dc=1)),
        send(z9s, z9r, dev(dc=1)),
    ]

    for d1 in (1, 3):
        for h in range(2):
            second_forward(h, d1)
    for h in range(2):
        second_forward(h, 2)

    for c in z2:
        c.wait_recv()
    thr = thr_ref[0, 0]
    for s, total in ((0, nine + (z2r[0, 0] + z2r[0, 1])), (1, z9r[...] + (z2r[1, 0] + z2r[1, 1]))):
        factor = thr / jnp.maximum(jnp.sqrt(total), thr)
        cols = slice(512 * s, 512 * s + 512)
        sct[:, cols] = (kgt[:, cols].astype(F32) * factor).astype(BF16)
    share_acts.wait_recv()

    def chip(dy, dx):
        return lax.rem(yy + dy, 4) * 4 + lax.rem(xx + dx, 4)

    def columns(dy, dx):
        return pl.ds(pl.multiple_of(128 * chip(dy, dx), 128), 128)

    def product(pair):
        out = None
        for s in range(2):
            rhs = jnp.concatenate([acts[s, :, columns(*q)] for q in pair], axis=1)
            part = jnp.dot(sct[:, 512 * s : 512 * s + 512], rhs, preferred_element_type=F32)
            out = part if out is None else out + part
        for i, (dy, dx) in enumerate(pair):
            for h in range(2):
                d1, d2 = (dx, dy) if h == 0 else (dy, dx)
                r = out[128 * h : 128 * h + 128, 128 * i : 128 * i + 128]
                p = POS[d2]
                if d1 == 0:
                    pf[h, p] = r
                elif d1 == 2:
                    pb[h, 1, p] = r.astype(BF16)
                elif d1 == 1:
                    pc[h, 0, p] = r[:64]
                    pb[h, 0, p, 64:] = r[64:].astype(BF16)
                else:
                    pb[h, 2, p, :64] = r[:64].astype(BF16)
                    pc[h, 1, p] = r[64:]

    s_a, s_b, s_c = {}, {}, {}

    def send_a(g):
        lo, hi = GROUPS[g]
        ps = pl.ds(lo, hi - lo)
        for h in range(2):
            s_a[h, g] = (
                send(pb.at[h, 1, ps, pl.ds(0, 64)], ra.at[h, 0, ps], step[h](1)),
                send(pb.at[h, 1, ps, pl.ds(64, 64)], ra.at[h, 1, ps], step[h](-1)),
            )

    def send_b(g):
        lo, hi = GROUPS[g]
        ps = pl.ds(lo, hi - lo)
        for h in range(2):
            s_b[h, g] = (
                send(pb.at[h, 0, ps, pl.ds(64, 64)], rx.at[h, 0, ps, pl.ds(64, 64)], step[h](1)),
                send(pb.at[h, 2, ps, pl.ds(0, 64)], rx.at[h, 1, ps, pl.ds(0, 64)], step[h](-1)),
            )

    def send_c(g):
        lo, hi = GROUPS[g]
        ps = pl.ds(lo, hi - lo)
        for h in range(2):
            pair = []
            for s in range(2):
                s_a[h, g][s].wait_recv()
                for p in range(lo, hi):
                    cb[h, s, p] = (pc[h, s, p] + ra[h, s, p].astype(F32)).astype(BF16)
                pair.append(
                    send(cb.at[h, s, ps], rx.at[h, s, ps, pl.ds(64 * s, 64)], step[h](1 - 2 * s))
                )
            s_c[h, g] = pair

    def gathered(g):
        lo, hi = GROUPS[g]
        for h in range(2):
            for s in range(2):
                s_b[h, g][s].wait_recv()
                s_c[h, g][s].wait_recv()
            for p in range(lo, hi):
                ss[h, p] = pf[h, p] + rx[h, 0, p].astype(F32) + rx[h, 1, p].astype(F32)

    product(((2, 2), (2, 1)))
    product(((2, 3), (1, 2)))
    send_a(0)
    product(((3, 2), (1, 1)))
    send_b(0)
    send_a(1)
    product(((1, 3), (3, 1)))
    product(((3, 3), (0, 2)))
    send_b(1)
    product(((2, 0), (0, 1)))
    send_a(2)
    product(((0, 3), (1, 0)))
    product(((3, 0), (0, 0)))
    send_b(2)
    send_c(0)

    for h in range(2):
        for d1 in range(4):
            for c in g_b2[h, d1]:
                c.wait_recv()
    share_w = [
        send(wr.at[dy, :, core], wr.at[dy, :, core], dev(dc=1)) for dy in range(4)
    ]

    send_c(1)
    gathered(0)
    p2a = [
        (
            send(ss.at[h, 0, pl.ds(0, 64)], ra2.at[h, 0], step[1 - h](1)),
            send(ss.at[h, 0, pl.ds(64, 64)], ra2.at[h, 1], step[1 - h](-1)),
        )
        for h in range(2)
    ]
    send_c(2)

    def act_rows(dy):
        share_w[dy].wait_recv()
        for dx in (0, 2):
            w = wr[dy, dx : dx + 2].reshape(256, KV)
            out = lax.dot_general(kg[...], w, NT, preferred_element_type=F32).astype(BF16)
            act_v[:, columns(dy, dx)] = out[:, :128]
            act_v[:, columns(dy, dx + 1)] = out[:, 128:]

    act_rows(0)
    act_rows(1)

    gathered(1)
    p2b = [
        (
            send(ss.at[h, 1, pl.ds(64, 64)], rx2.at[h, 0, pl.ds(64, 64)], step[1 - h](1)),
            send(ss.at[h, 2, pl.ds(0, 64)], rx2.at[h, 1, pl.ds(0, 64)], step[1 - h](-1)),
        )
        for h in range(2)
    ]
    p2c = []
    for h in range(2):
        for s in range(2):
            p2a[h][s].wait_recv()
            cb2[h, s] = ss[h, 1 + s, 64 * s : 64 * s + 64] + ra2[h, s]
            p2c.append(send(cb2.at[h, s], rx2.at[h, s, pl.ds(64 * s, 64)], step[1 - h](1 - 2 * s)))

    act_rows(2)
    act_rows(3)
    store = pltpu.make_async_copy(act_v, act_out, lsem.at[3])
    store.start()

    gathered(2)
    for h in range(2):
        for s in range(2):
            p2b[h][s].wait_recv()
            p2c[2 * h + s].wait_recv()
        tb[:, 128 * h : 128 * h + 128] = (ss[h, 3] + rx2[h, 0] + rx2[h, 1]).T
    swap = send(tb.at[pl.ds(pl.multiple_of(64 * (1 - core), 64), 64)], wsw, dev(dc=1))
    wg_out[:, pl.ds(own, 256)] = tb[pl.ds(pl.multiple_of(64 * core, 64), 64)]
    swap.wait_recv()
    wg_out[:, pl.ds(pl.multiple_of(256 * (1 - core), 256), 256)] = wsw[...]
    store.wait()
    assert len(started) == N_SEMS
    for c in started:
        c.wait_send()


def shards(acts, key_grads, key_weight, lengths, threshold):
    hbm = pl.BlockSpec(memory_space=pl.ANY)
    smem = pl.BlockSpec(memory_space=pltpu.SMEM)
    v = pltpu.VMEM
    act_part, weight_part = pl.pallas_call(
        kernel,
        out_shape=(
            jax.ShapeDtypeStruct((TOK, D), BF16),
            jax.ShapeDtypeStruct((D // 32, KV), F32),
        ),
        in_specs=[hbm, hbm, hbm, smem, smem],
        out_specs=(hbm, pl.BlockSpec(memory_space=v)),
        scratch_shapes=[
            v((2, TOK, D), BF16),
            v((TOK, KV), BF16),
            v((TOK, 256), BF16),
            v((256, 2 * TOK), BF16),
            v((256, 2 * TOK), BF16),
            v((4, 4, 2, 64, KV), BF16),
            v((TOK, D), BF16),
            v((1, TOK), F32),
            v((8, 1, TOK), F32),
            v((2, 1, TOK), F32),
            v((2, 2, 1, TOK), F32),
            v((1, TOK), F32),
            v((1, TOK), F32),
            v((2, 3, 4, 128, 128), BF16),
            v((2, 2, 4, 64, 128), F32),
            v((2, 4, 128, 128), F32),
            v((2, 2, 4, 64, 128), BF16),
            v((2, 2, 4, 64, 128), BF16),
            v((2, 2, 4, 128, 128), BF16),
            v((2, 4, 128, 128), F32),
            v((2, 2, 64, 128), F32),
            v((2, 2, 64, 128), F32),
            v((2, 2, 128, 128), F32),
            v((128, 256), F32),
            v((64, 256), F32),
            pltpu.SemaphoreType.DMA((N_SEMS,)),
            pltpu.SemaphoreType.DMA((N_SEMS,)),
            pltpu.SemaphoreType.DMA((4,)),
        ],
        compiler_params=pltpu.CompilerParams(
            collective_id=0, has_side_effects=True, vmem_limit_bytes=48 * 2**20
        ),
    )(acts[0], key_grads[0], key_weight[0], lengths, threshold.reshape(1, 1))
    return (act_part[None], weight_part[None])


def solution(mesh):
    in_specs = (
        P("section", "dp", None),
        P("section", "dp", None),
        P("section", "dp", None),
        P("dp", None),
        P(),
    )
    out_specs = (P("section", "dp", None), P("section", "dp", None))
    return jax.shard_map(shards, mesh=mesh, in_specs=in_specs, out_specs=out_specs, check_vma=False)
```

time: 192 us -> 54.6 us (0.28)
  waiting for transfers between devices: 127 us -> 0 us
  Pallas kernels: 0 us -> 46.9 us
  blocking collectives: 31.2 us -> 0 us
  between operations: 14.7 us -> 1.3 us
  matrix products: 10.5 us -> 0 us
    unnamed x3 -> x0, waiting for transfers between devices: 103 us -> none
    pallas_call x0 -> x1, Pallas kernels: none -> 46.9 us  [shards(): pl.pallas_call(kernel, out_shape=(jax.ShapeDtypeStruct((TOK, D), BF16), j...]
    psum x1 -> x0, blocking collectives: 31.2 us -> none  [shards(): total = lax.psum(squares, 'section')]
    all_gather x1 -> x0, waiting for transfers between devices: 23.3 us -> none  [shards(): lax.all_gather(key_weight[0], 'dp', axis=0, tiled=True)]
    dot_general x4 -> x0, matrix products: 10.5 us -> none  [the longest x1 4.19 us: shards(): lax.dot_general(grads, lax.all_gather(key_weight[0], 'dp', axis=0, tiled=...]
    unnamed x7 -> x10, local copies, waits for them, and re-layouts: 7.17 us -> 6.1 us
  transfers between devices with their start and end apart: 2 -> 0, of which waited for: 2 -> 0; matrix products, arithmetic and copies ran while one was open for 9% -> 0% of each run, Pallas kernels for 0% -> 0%
where the time goes in v1:
time: 54.6 us; the launch traced here: 54.3 us
  Pallas kernels  46.9 us (86%)
  local copies, waits for them, and re-layouts  6.1 us (11%)
  between operations  1.3 us (2%)
    pallas_call x1, Pallas kernels, shards(): pl.pallas_call(kernel, out_shape=(jax.ShapeDtypeStruct((TOK, D), BF16), j...  46.9 us
    unnamed x10, local copies, waits for them, and re-layouts  6.1 us

profile of v1, /device:TPU:1, one launch (start us, length us, event | category | flops | bytes accessed | tf_op | source)
XLA Modules:
  0.0 54.3 jit_solution(12343324394931270724)
XLA Ops:
  1.3 0.0 copy-start
  1.3 1.6 %copy-done = bf16[1,512,2048]{2,1,0:T(8,128)(2,1)S(1)} copy-done((bf16[1,512,2048]{2,1,0:T(8,128)(2,1)S(1)}, bf16[1,512,2048]{2,1,0:T(8,128)(2,1)}, u32[]{:S(2)}) %copy-start) | copy-done | bytes 2097176
  2.9 0.0 copy-start.1
  2.9 1.0 %copy-done.1 = bf16[1,512,512]{2,1,0:T(8,128)(2,1)S(1)} copy-done((bf16[1,512,512]{2,1,0:T(8,128)(2,1)S(1)}, bf16[1,512,512]{2,1,0:T(8,128)(2,1)}, u32[]{:S(2)}) %copy-start.1) | copy-done | bytes 524312
  3.9 0.0 copy-start.2
  3.9 0.8 %copy-done.2 = bf16[1,64,512]{2,1,0:T(8,128)(2,1)S(1)} copy-done((bf16[1,64,512]{2,1,0:T(8,128)(2,1)S(1)}, bf16[1,64,512]{2,1,0:T(8,128)(2,1)}, u32[]{:S(2)}) %copy-start.2) | copy-done | bytes 65560
  4.8 0.0 copy-start.3
  4.8 0.7 %copy-done.3 = s32[1,16]{1,0:T(1,128)S(1)} copy-done((s32[1,16]{1,0:T(1,128)S(1)}, s32[1,16]{1,0:T(1,128)}, u32[]{:S(2)}) %copy-start.3) | copy-done | bytes 88
  5.4 46.9 %shard_map.68 = (bf16[512,2048]{1,0:T(8,128)(2,1)S(1)}, f32[64,512]{1,0:T(8,128)S(1)}) custom-call(bf16[512,2048]{1,0:T(8,128)(2,1)S(1)} %bitcast.7, bf16[512,512]{1,0:T(8,128)(2,1)S(1)} %bitcast.9, bf16[64,512]{1,0:T(8,128)(2,1)S(1)} %bitcast.11, s32[1,16]{1,0:T(1,128)S(1)} %copy-done.3, f32[1,1]{1,0:T(1,128)} %bitcast.6.thr_ref), custom_call_target="tpu_custom_call" | custom-call | tf_op jit(solution)/shard_map/pallas_call | solution.py:347
  52.3 1.3 %copy.10 = bf16[1,512,2048]{2,1,0:T(8,128)(2,1)} copy(bf16[1,512,2048]{2,1,0:T(8,128)(2,1)S(1)} %bitcast.8) | data formatting | bytes 4194304
  53.7 0.7 %copy.11 = f32[1,64,512]{2,1,0:T(8,128)} copy(f32[1,64,512]{2,1,0:T(8,128)S(1)} %bitcast.10) | data formatting | bytes 262144
Async XLA Ops:
  1.3 1.6 %copy-start = (bf16[1,512,2048]{2,1,0:T(8,128)(2,1)S(1)}, bf16[1,512,2048]{2,1,0:T(8,128)(2,1)}, u32[]{:S(2)}) copy-start(bf16[1,512,2048]{2,1,0:T(8,128)(2,1)} %param.5) | copy-start | bytes 6291460
  2.9 1.0 %copy-start.1 = (bf16[1,512,512]{2,1,0:T(8,128)(2,1)S(1)}, bf16[1,512,512]{2,1,0:T(8,128)(2,1)}, u32[]{:S(2)}) copy-start(bf16[1,512,512]{2,1,0:T(8,128)(2,1)} %param.6) | copy-start | bytes 1572868
  3.9 0.8 %copy-start.2 = (bf16[1,64,512]{2,1,0:T(8,128)(2,1)S(1)}, bf16[1,64,512]{2,1,0:T(8,128)(2,1)}, u32[]{:S(2)}) copy-start(bf16[1,64,512]{2,1,0:T(8,128)(2,1)} %param.7) | copy-start | bytes 196612
  4.8 0.7 %copy-start.3 = (s32[1,16]{1,0:T(1,128)S(1)}, s32[1,16]{1,0:T(1,128)}, u32[]{:S(2)}) copy-start(s32[1,16]{1,0:T(1,128)} %len_ref.1) | copy-start | bytes 196

commit v2 on v1

--- a/solution.py
+++ b/solution.py
@@ -45,10 +45,12 @@
         return copy
 
     load_kg = pltpu.make_async_copy(kg_hbm, kg, lsem.at[0])
-    load_acts = pltpu.make_async_copy(acts_hbm, acts.at[0], lsem.at[1])
-    load_w = pltpu.make_async_copy(w_hbm, wr.at[0, 0, core], lsem.at[2])
+    load_lo = pltpu.make_async_copy(acts_hbm.at[0:256], acts.at[0, 0:256], lsem.at[1])
+    load_hi = pltpu.make_async_copy(acts_hbm.at[256:512], acts.at[0, 256:512], lsem.at[2])
+    load_w = pltpu.make_async_copy(w_hbm, wr.at[0, 0, core], lsem.at[3])
     load_kg.start()
-    load_acts.start()
+    load_lo.start()
+    load_hi.start()
     load_w.start()
 
     near = [dev(dc=1), dev(dx=1), dev(dx=-1), dev(dy=1), dev(dy=-1)]
@@ -57,6 +59,46 @@
     barrier = pltpu.get_barrier_semaphore()
     for who in partners:
         pl.semaphore_signal(barrier, inc=1, device_id=who, device_id_type=MESH)
+
+    pl.semaphore_wait(barrier, len(partners))
+
+    step = (lambda s: dev(dx=s), lambda s: dev(dy=s))
+
+    def at(h, d1, d2):
+        return (d2, d1) if h == 0 else (d1, d2)
+
+    def slot(h, d1, d2, lo=0, hi=32):
+        return wr.at[(*at(h, d1, d2), core, pl.ds(32 * h + lo, hi - lo))]
+
+    g_a1, g_a2, g_b1, g_b2 = {}, {}, {}, {}
+    for h in range(2):
+        mine = w_hbm.at[pl.ds(32 * h, 32)]
+        g_a1[h] = (
+            send(mine, slot(h, 3, 0), step[h](1)),
+            send(mine, slot(h, 1, 0), step[h](-1)),
+        )
+
+    def second(h, d1):
+        mine = slot(h, d1, 0) if d1 else w_hbm.at[pl.ds(32 * h, 32)]
+        return (
+            send(mine, slot(h, d1, 3), step[1 - h](1)),
+            send(mine, slot(h, d1, 1), step[1 - h](-1)),
+        )
+
+    def second_forward(h, d1):
+        for c in g_b1[h, d1]:
+            c.wait_recv()
+        g_b2[h, d1] = (
+            send(slot(h, d1, 3, 0, 16), slot(h, d1, 2, 0, 16), step[1 - h](1)),
+            send(slot(h, d1, 1, 16, 32), slot(h, d1, 2, 16, 32), step[1 - h](-1)),
+        )
+
+    for h in range(2):
+        g_b1[h, 0] = second(h, 0)
+    share_kg = send(
+        kg_hbm.at[:, pl.ds(pl.multiple_of(256 * (1 - core), 256), 256)], kgs, dev(dc=1)
+    )
+    share_acts = send(acts_hbm, acts.at[1], dev(dc=1))
 
     lane = lax.broadcasted_iota(jnp.int32, (1, TOK), 1)
     sub = lax.broadcasted_iota(jnp.int32, (TOK, 1), 0)
@@ -68,8 +110,6 @@
         seg_row = seg_row + (lane >= end).astype(jnp.int32)
         seg_col = seg_col + (sub >= end).astype(jnp.int32)
 
-    load_kg.wait()
-    load_acts.wait()
 
     def masked(rows, cols):
         (r0, r1), (c0, c1) = rows, cols
@@ -81,7 +121,10 @@
     def spread(same, r):
         return jnp.sum(jnp.where(same, r, 0.0), axis=0, keepdims=True)
 
+    load_kg.wait()
+    load_lo.wait()
     same_a, r_a = masked((0, 256), (0, 256))
+    load_hi.wait()
     same_c, r_c = masked((128, 256), (256, 384))
     same_b, r_b = masked((256, 512), (256, 512))
     r_1 = r_a[128:] + 2.0 * r_c
@@ -93,46 +136,7 @@
     zv[:, 256:384] = v_b[:, 0:128] + spread(same_c, r_1)
     zv[:, 384:512] = v_b[:, 128:256]
 
-    pl.semaphore_wait(barrier, len(partners))
-
     z1 = [send(zv, zr.at[i], dev(dz=k)) for i, k in enumerate(zs)]
-
-    load_w.wait()
-    step = (lambda s: dev(dx=s), lambda s: dev(dy=s))
-
-    def at(h, d1, d2):
-        return (d2, d1) if h == 0 else (d1, d2)
-
-    def slot(h, d1, d2, lo=0, hi=32):
-        return wr.at[(*at(h, d1, d2), core, pl.ds(32 * h + lo, hi - lo))]
-
-    g_a1, g_a2, g_b1, g_b2 = {}, {}, {}, {}
-    for h in range(2):
-        g_a1[h] = (
-            send(slot(h, 0, 0), slot(h, 3, 0), step[h](1)),
-            send(slot(h, 0, 0), slot(h, 1, 0), step[h](-1)),
-        )
-    share_kg = send(
-        kg.at[:, pl.ds(pl.multiple_of(256 * (1 - core), 256), 256)], kgs, dev(dc=1)
-    )
-    share_acts = send(acts.at[0], acts.at[1], dev(dc=1))
-
-    def second(h, d1):
-        return (
-            send(slot(h, d1, 0), slot(h, d1, 3), step[1 - h](1)),
-            send(slot(h, d1, 0), slot(h, d1, 1), step[1 - h](-1)),
-        )
-
-    def second_forward(h, d1):
-        for c in g_b1[h, d1]:
-            c.wait_recv()
-        g_b2[h, d1] = (
-            send(slot(h, d1, 3, 0, 16), slot(h, d1, 2, 0, 16), step[1 - h](1)),
-            send(slot(h, d1, 1, 16, 32), slot(h, d1, 2, 16, 32), step[1 - h](-1)),
-        )
-
-    for h in range(2):
-        g_b1[h, 0] = second(h, 0)
 
     own = pl.multiple_of(256 * core, 256)
     kgt[:, 0:512] = kg[:, pl.ds(own, 256)].T
@@ -156,27 +160,40 @@
     share_kg.wait_recv()
     kgt[:, 512:1024] = kgs[...].T
 
-    for c in z1:
+    for c in z1[0::2]:
         c.wait_recv()
-    up = zr[0] + zr[2] + zr[4]
-    down = zr[1] + zr[3] + zr[5]
-    z2s[0] = up + zr[6]
-    z2s[1] = down
-    nine = zv[...] + (up + down) + (zr[6] + zr[7])
-    z9s[...] = nine
+    up = zr[0] + zr[2] + zr[4] + zr[6]
+    z2s[0] = up
     z2 = [
         send(z2s.at[0], z2r.at[0, 0], dev(dz=4)),
+        send(z2s.at[0], z2r.at[1, 0], dev(dz=4, dc=1)),
+    ]
+    for c in z1[1::2]:
+        c.wait_recv()
+    down = zr[1] + zr[3] + zr[5]
+    z2s[1] = down
+    z2 += [
         send(z2s.at[1], z2r.at[0, 1], dev(dz=-4)),
-        send(z2s.at[0], z2r.at[1, 0], dev(dz=4, dc=1)),
         send(z2s.at[1], z2r.at[1, 1], dev(dz=-4, dc=1)),
-        send(z9s, z9r, dev(dc=1)),
     ]
+    nine = zv[...] + up + (down + zr[7])
+    z9s[...] = nine
+    z2.append(send(z9s, z9r, dev(dc=1)))
 
     for d1 in (1, 3):
         for h in range(2):
             second_forward(h, d1)
     for h in range(2):
         second_forward(h, 2)
+
+    load_w.wait()
+    for h in range(2):
+        for d1 in range(4):
+            for c in g_b2[h, d1]:
+                c.wait_recv()
+    share_w = [
+        send(wr.at[dy, :, core], wr.at[dy, :, core], dev(dc=1)) for dy in range(4)
+    ]
 
     for c in z2:
         c.wait_recv()
@@ -274,14 +291,6 @@
     send_b(2)
     send_c(0)
 
-    for h in range(2):
-        for d1 in range(4):
-            for c in g_b2[h, d1]:
-                c.wait_recv()
-    share_w = [
-        send(wr.at[dy, :, core], wr.at[dy, :, core], dev(dc=1)) for dy in range(4)
-    ]
-
     send_c(1)
     gathered(0)
     p2a = [
@@ -321,7 +330,7 @@
 
     act_rows(2)
     act_rows(3)
-    store = pltpu.make_async_copy(act_v, act_out, lsem.at[3])
+    store = pltpu.make_async_copy(act_v, act_out, lsem.at[4])
     store.start()
 
     gathered(2)
@@ -341,7 +350,8 @@
 
 
 def shards(acts, key_grads, key_weight, lengths, threshold):
-    hbm = pl.BlockSpec(memory_space=pl.ANY)
+    hbm = pl.BlockSpec(memory_space=pltpu.HBM)
+    anywhere = pl.BlockSpec(memory_space=pl.ANY)
     smem = pl.BlockSpec(memory_space=pltpu.SMEM)
     v = pltpu.VMEM
     act_part, weight_part = pl.pallas_call(
@@ -351,7 +361,7 @@
             jax.ShapeDtypeStruct((D // 32, KV), F32),
         ),
         in_specs=[hbm, hbm, hbm, smem, smem],
-        out_specs=(hbm, pl.BlockSpec(memory_space=v)),
+        out_specs=(anywhere, pl.BlockSpec(memory_space=v)),
         scratch_shapes=[
             v((2, TOK, D), BF16),
             v((TOK, KV), BF16),
@@ -380,7 +390,7 @@
             v((64, 256), F32),
             pltpu.SemaphoreType.DMA((N_SEMS,)),
             pltpu.SemaphoreType.DMA((N_SEMS,)),
-            pltpu.SemaphoreType.DMA((4,)),
+            pltpu.SemaphoreType.DMA((5,)),
         ],
         compiler_params=pltpu.CompilerParams(
             collective_id=0, has_side_effects=True, vmem_limit_bytes=48 * 2**20

time: 54.6 us -> 55.9 us (1.024)
  Pallas kernels: 46.9 us -> 48.2 us
    pallas_call x1, Pallas kernels: 46.9 us -> 48.2 us  [shards(): pl.pallas_call(kernel, out_shape=(jax.ShapeDtypeStruct((TOK, D), BF16), j...]
where the time goes in v2:
time: 55.9 us; the launch traced here: 55.6 us
  Pallas kernels  48.2 us (86%)
  local copies, waits for them, and re-layouts  6.1 us (11%)
  between operations  1.3 us (2%)
    pallas_call x1, Pallas kernels, shards(): pl.pallas_call(kernel, out_shape=(jax.ShapeDtypeStruct((TOK, D), BF16), j...  48.2 us
    unnamed x10, local copies, waits for them, and re-layouts  6.1 us

profile of v2, /device:TPU:1, one launch (start us, length us, event | category | flops | bytes accessed | tf_op | source)
XLA Modules:
  0.0 55.6 jit_solution(18381580035276645518)
XLA Ops:
  1.3 0.0 copy-start
  1.3 1.6 %copy-done = bf16[1,512,2048]{2,1,0:T(8,128)(2,1)S(1)} copy-done((bf16[1,512,2048]{2,1,0:T(8,128)(2,1)S(1)}, bf16[1,512,2048]{2,1,0:T(8,128)(2,1)}, u32[]{:S(2)}) %copy-start) | copy-done | bytes 2097176
  2.9 0.0 copy-start.1
  2.9 1.0 %copy-done.1 = bf16[1,512,512]{2,1,0:T(8,128)(2,1)S(1)} copy-done((bf16[1,512,512]{2,1,0:T(8,128)(2,1)S(1)}, bf16[1,512,512]{2,1,0:T(8,128)(2,1)}, u32[]{:S(2)}) %copy-start.1) | copy-done | bytes 524312
  3.9 0.0 copy-start.2
  3.9 0.8 %copy-done.2 = bf16[1,64,512]{2,1,0:T(8,128)(2,1)S(1)} copy-done((bf16[1,64,512]{2,1,0:T(8,128)(2,1)S(1)}, bf16[1,64,512]{2,1,0:T(8,128)(2,1)}, u32[]{:S(2)}) %copy-start.2) | copy-done | bytes 65560
  4.8 0.0 copy-start.3
  4.8 0.7 %copy-done.3 = s32[1,16]{1,0:T(1,128)S(1)} copy-done((s32[1,16]{1,0:T(1,128)S(1)}, s32[1,16]{1,0:T(1,128)}, u32[]{:S(2)}) %copy-start.3) | copy-done | bytes 88
  5.4 48.2 %shard_map.68 = (bf16[512,2048]{1,0:T(8,128)(2,1)S(1)}, f32[64,512]{1,0:T(8,128)S(1)}) custom-call(bf16[512,2048]{1,0:T(8,128)(2,1)S(1)} %bitcast.7, bf16[512,512]{1,0:T(8,128)(2,1)S(1)} %bitcast.9, bf16[64,512]{1,0:T(8,128)(2,1)S(1)} %bitcast.11, s32[1,16]{1,0:T(1,128)S(1)} %copy-done.3, f32[1,1]{1,0:T(1,128)} %bitcast.6.thr_ref), custom_call_target="tpu_custom_call" | custom-call | tf_op jit(solution)/shard_map/pallas_call | solution.py:357
  53.6 1.3 %copy.10 = bf16[1,512,2048]{2,1,0:T(8,128)(2,1)} copy(bf16[1,512,2048]{2,1,0:T(8,128)(2,1)S(1)} %bitcast.8) | data formatting | bytes 4194304
  55.0 0.7 %copy.11 = f32[1,64,512]{2,1,0:T(8,128)} copy(f32[1,64,512]{2,1,0:T(8,128)S(1)} %bitcast.10) | data formatting | bytes 262144
Async XLA Ops:
  1.3 1.6 %copy-start = (bf16[1,512,2048]{2,1,0:T(8,128)(2,1)S(1)}, bf16[1,512,2048]{2,1,0:T(8,128)(2,1)}, u32[]{:S(2)}) copy-start(bf16[1,512,2048]{2,1,0:T(8,128)(2,1)} %param.5) | copy-start | bytes 6291460
  2.9 1.0 %copy-start.1 = (bf16[1,512,512]{2,1,0:T(8,128)(2,1)S(1)}, bf16[1,512,512]{2,1,0:T(8,128)(2,1)}, u32[]{:S(2)}) copy-start(bf16[1,512,512]{2,1,0:T(8,128)(2,1)} %param.6) | copy-start | bytes 1572868
  3.9 0.8 %copy-start.2 = (bf16[1,64,512]{2,1,0:T(8,128)(2,1)S(1)}, bf16[1,64,512]{2,1,0:T(8,128)(2,1)}, u32[]{:S(2)}) copy-start(bf16[1,64,512]{2,1,0:T(8,128)(2,1)} %param.7) | copy-start | bytes 196612
  4.8 0.7 %copy-start.3 = (s32[1,16]{1,0:T(1,128)S(1)}, s32[1,16]{1,0:T(1,128)}, u32[]{:S(2)}) copy-start(s32[1,16]{1,0:T(1,128)} %len_ref.1) | copy-start | bytes 196

commit v3 on v2

--- a/solution.py
+++ b/solution.py
@@ -11,15 +11,16 @@
 D, KV, TOK, PAT = 2048, 512, 512, 16
 POS = {2: 0, 1: 1, 3: 2, 0: 3}
 GROUPS = ((0, 1), (1, 3), (3, 4))
-N_SEMS = 108
+N_SEMS = 109
+VMEM = 58000 * 1024
 
 
 def kernel(
     acts_hbm, kg_hbm, w_hbm, len_ref, thr_ref, act_out, wg_out,
     acts, kg, kgs, kgt, sct, wr, act_v,
     zv, zr, z2s, z2r, z9s, z9r,
-    pb, pc, pf, ra, cb, rx, ss, ra2, cb2, rx2, tb, wsw,
-    ssem, rsem, lsem,
+    pb, pc, pf, ra, cb, rx, ss, ra2, cb2, rx2, wsw,
+    ssem, rsem, wsem, lsem,
 ):
     z = lax.axis_index("section")
     dp = lax.axis_index("dp")
@@ -27,18 +28,20 @@
     xx = lax.rem(lax.div(dp, 2), 4)
     yy = lax.div(dp, 8)
 
-    def dev(dy=0, dx=0, dc=0, dz=0):
+    def dev(dy=0, dx=0, dc=0, dz=0, at_core=None):
         y2, x2 = lax.rem(yy + dy + 4, 4), lax.rem(xx + dx + 4, 4)
         c2 = 1 - core if dc else core
+        if at_core is not None:
+            c2 = at_core
         return (lax.rem(z + dz + 16, 16), (y2 * 4 + x2) * 2 + c2)
 
     started = []
 
-    def send(src, dst, to):
+    def send(src, dst, to, arrival=None):
         k = len(started)
         copy = pltpu.make_async_remote_copy(
-            src_ref=src, dst_ref=dst, send_sem=ssem.at[k], recv_sem=rsem.at[k],
-            device_id=to, device_id_type=MESH,
+            src_ref=src, dst_ref=dst, send_sem=ssem.at[k],
+            recv_sem=rsem.at[k] if arrival is None else arrival, device_id=to, device_id_type=MESH,
         )
         copy.start()
         started.append(copy)
@@ -59,46 +62,6 @@
     barrier = pltpu.get_barrier_semaphore()
     for who in partners:
         pl.semaphore_signal(barrier, inc=1, device_id=who, device_id_type=MESH)
-
-    pl.semaphore_wait(barrier, len(partners))
-
-    step = (lambda s: dev(dx=s), lambda s: dev(dy=s))
-
-    def at(h, d1, d2):
-        return (d2, d1) if h == 0 else (d1, d2)
-
-    def slot(h, d1, d2, lo=0, hi=32):
-        return wr.at[(*at(h, d1, d2), core, pl.ds(32 * h + lo, hi - lo))]
-
-    g_a1, g_a2, g_b1, g_b2 = {}, {}, {}, {}
-    for h in range(2):
-        mine = w_hbm.at[pl.ds(32 * h, 32)]
-        g_a1[h] = (
-            send(mine, slot(h, 3, 0), step[h](1)),
-            send(mine, slot(h, 1, 0), step[h](-1)),
-        )
-
-    def second(h, d1):
-        mine = slot(h, d1, 0) if d1 else w_hbm.at[pl.ds(32 * h, 32)]
-        return (
-            send(mine, slot(h, d1, 3), step[1 - h](1)),
-            send(mine, slot(h, d1, 1), step[1 - h](-1)),
-        )
-
-    def second_forward(h, d1):
-        for c in g_b1[h, d1]:
-            c.wait_recv()
-        g_b2[h, d1] = (
-            send(slot(h, d1, 3, 0, 16), slot(h, d1, 2, 0, 16), step[1 - h](1)),
-            send(slot(h, d1, 1, 16, 32), slot(h, d1, 2, 16, 32), step[1 - h](-1)),
-        )
-
-    for h in range(2):
-        g_b1[h, 0] = second(h, 0)
-    share_kg = send(
-        kg_hbm.at[:, pl.ds(pl.multiple_of(256 * (1 - core), 256), 256)], kgs, dev(dc=1)
-    )
-    share_acts = send(acts_hbm, acts.at[1], dev(dc=1))
 
     lane = lax.broadcasted_iota(jnp.int32, (1, TOK), 1)
     sub = lax.broadcasted_iota(jnp.int32, (TOK, 1), 0)
@@ -136,7 +99,47 @@
     zv[:, 256:384] = v_b[:, 0:128] + spread(same_c, r_1)
     zv[:, 384:512] = v_b[:, 128:256]
 
+    pl.semaphore_wait(barrier, len(partners))
     z1 = [send(zv, zr.at[i], dev(dz=k)) for i, k in enumerate(zs)]
+
+    step = (lambda s, c=None: dev(dx=s, at_core=c), lambda s, c=None: dev(dy=s, at_core=c))
+
+    def at(h, d1, d2):
+        return (d2, d1) if h == 0 else (d1, d2)
+
+    def slot(h, d1, d2, lo=0, hi=32):
+        return wr.at[(*at(h, d1, d2), core, pl.ds(32 * h + lo, hi - lo))]
+
+    g_a1, g_a2, g_b1, g_b2 = {}, {}, {}, {}
+    for h in range(2):
+        mine = w_hbm.at[pl.ds(32 * h, 32)]
+        g_a1[h] = (
+            send(mine, slot(h, 3, 0), step[h](1)),
+            send(mine, slot(h, 1, 0), step[h](-1)),
+        )
+
+    def second(h, d1):
+        mine = slot(h, d1, 0) if d1 else w_hbm.at[pl.ds(32 * h, 32)]
+        return (
+            send(mine, slot(h, d1, 3), step[1 - h](1)),
+            send(mine, slot(h, d1, 1), step[1 - h](-1)),
+        )
+
+    def second_forward(h, d1):
+        for c in g_b1[h, d1]:
+            c.wait_recv()
+        g_b2[h, d1] = (
+            send(slot(h, d1, 3, 0, 16), slot(h, d1, 2, 0, 16), step[1 - h](1)),
+            send(slot(h, d1, 1, 16, 32), slot(h, d1, 2, 16, 32), step[1 - h](-1)),
+        )
+
+    for h in range(2):
+        g_b1[h, 0] = second(h, 0)
+    share_kg = send(
+        kg_hbm.at[:, pl.ds(pl.multiple_of(256 * (1 - core), 256), 256)], kgs, dev(dc=1)
+    )
+    share_acts = send(acts_hbm, acts.at[1], dev(dc=1))
+
 
     own = pl.multiple_of(256 * core, 256)
     kgt[:, 0:512] = kg[:, pl.ds(own, 256)].T
@@ -273,7 +276,7 @@
                 s_b[h, g][s].wait_recv()
                 s_c[h, g][s].wait_recv()
             for p in range(lo, hi):
-                ss[h, p] = pf[h, p] + rx[h, 0, p].astype(F32) + rx[h, 1, p].astype(F32)
+                ss[h, p] = (pf[h, p] + rx[h, 0, p].astype(F32) + rx[h, 1, p].astype(F32)).T
 
     product(((2, 2), (2, 1)))
     product(((2, 3), (1, 2)))
@@ -314,19 +317,17 @@
     act_rows(1)
 
     gathered(1)
-    p2b = [
-        (
-            send(ss.at[h, 1, pl.ds(64, 64)], rx2.at[h, 0, pl.ds(64, 64)], step[1 - h](1)),
-            send(ss.at[h, 2, pl.ds(0, 64)], rx2.at[h, 1, pl.ds(0, 64)], step[1 - h](-1)),
-        )
-        for h in range(2)
-    ]
-    p2c = []
+    def last(src, h, s, c):
+        return send(src, rx2.at[core, h, s], step[1 - h](1 - 2 * s, c), wsem.at[core, h, s])
+
+    for h in range(2):
+        last(ss.at[h, 1, pl.ds(64, 64)], h, 0, 1)
+        last(ss.at[h, 2, pl.ds(0, 64)], h, 1, 0)
     for h in range(2):
         for s in range(2):
             p2a[h][s].wait_recv()
             cb2[h, s] = ss[h, 1 + s, 64 * s : 64 * s + 64] + ra2[h, s]
-            p2c.append(send(cb2.at[h, s], rx2.at[h, s, pl.ds(64 * s, 64)], step[1 - h](1 - 2 * s)))
+            last(cb2.at[h, s], h, s, s)
 
     act_rows(2)
     act_rows(3)
@@ -334,19 +335,45 @@
     store.start()
 
     gathered(2)
-    for h in range(2):
-        for s in range(2):
-            p2b[h][s].wait_recv()
-            p2c[2 * h + s].wait_recv()
-        tb[:, 128 * h : 128 * h + 128] = (ss[h, 3] + rx2[h, 0] + rx2[h, 1]).T
-    swap = send(tb.at[pl.ds(pl.multiple_of(64 * (1 - core), 64), 64)], wsw, dev(dc=1))
-    wg_out[:, pl.ds(own, 256)] = tb[pl.ds(pl.multiple_of(64 * core, 64), 64)]
-    swap.wait_recv()
-    wg_out[:, pl.ds(pl.multiple_of(256 * (1 - core), 256), 256)] = wsw[...]
+    given = [
+        send(ss.at[h, 3, pl.ds(pl.multiple_of(64 * (1 - core), 64), 64)], wsw.at[h], dev(dc=1))
+        for h in range(2)
+    ]
+    for h in range(2):
+        given[h].wait_recv()
+    for c in range(2):
+        for h in range(2):
+            for s in range(2):
+                pltpu.make_async_remote_copy(
+                    src_ref=cb2.at[h, s], dst_ref=rx2.at[c, h, s], send_sem=ssem.at[0],
+                    recv_sem=wsem.at[c, h, s], device_id=dev(dc=1), device_id_type=MESH,
+                ).wait_recv()
+    mine = pl.ds(pl.multiple_of(64 * core, 64), 64)
+    for h in range(2):
+        near = pl.ds(pl.multiple_of(256 * core + 128 * h, 128), 128)
+        far = pl.ds(pl.multiple_of(256 * (1 - core) + 128 * h, 128), 128)
+        wg_out[:, near] = ss[h, 3, mine] + rx2[core, h, 0] + rx2[core, h, 1]
+        wg_out[:, far] = wsw[h] + rx2[1 - core, h, 0] + rx2[1 - core, h, 1]
     store.wait()
     assert len(started) == N_SEMS
     for c in started:
         c.wait_send()
+
+
+def finish(act_in, wg_in, act_out, wg_out, act_v, wg_v, sems):
+    parts = [(wg_in, wg_v, wg_out)]
+    for k in range(8):
+        rows = pl.ds(64 * k, 64)
+        parts.append((act_in.at[rows], act_v.at[rows], act_out.at[rows]))
+    loads = [pltpu.make_async_copy(a, b, sems.at[0, k]) for k, (a, b, _) in enumerate(parts)]
+    stores = [pltpu.make_async_copy(b, c, sems.at[1, k]) for k, (_, b, c) in enumerate(parts)]
+    for c in loads:
+        c.start()
+    for c, d in zip(loads, stores):
+        c.wait()
+        d.start()
+    for d in stores:
+        d.wait()
 
 
 def shards(acts, key_grads, key_weight, lengths, threshold):
@@ -385,17 +412,28 @@
             v((2, 4, 128, 128), F32),
             v((2, 2, 64, 128), F32),
             v((2, 2, 64, 128), F32),
-            v((2, 2, 128, 128), F32),
-            v((128, 256), F32),
-            v((64, 256), F32),
+            v((2, 2, 2, 64, 128), F32),
+            v((2, 64, 128), F32),
             pltpu.SemaphoreType.DMA((N_SEMS,)),
             pltpu.SemaphoreType.DMA((N_SEMS,)),
+            pltpu.SemaphoreType.DMA((2, 2, 2)),
             pltpu.SemaphoreType.DMA((5,)),
         ],
         compiler_params=pltpu.CompilerParams(
-            collective_id=0, has_side_effects=True, vmem_limit_bytes=48 * 2**20
+            collective_id=0, has_side_effects=True, vmem_limit_bytes=VMEM
         ),
     )(acts[0], key_grads[0], key_weight[0], lengths, threshold.reshape(1, 1))
+    act_part, weight_part = pl.pallas_call(
+        finish,
+        out_shape=(
+            jax.ShapeDtypeStruct((TOK, D), BF16),
+            jax.ShapeDtypeStruct((D // 32, KV), F32),
+        ),
+        in_specs=[hbm, hbm],
+        out_specs=(hbm, hbm),
+        scratch_shapes=[v((TOK, D), BF16), v((D // 32, KV), F32), pltpu.SemaphoreType.DMA((2, 9))],
+        compiler_params=pltpu.CompilerParams(vmem_limit_bytes=VMEM),
+    )(act_part, weight_part)
     return (act_part[None], weight_part[None])
 
 

time: 55.9 us -> 50.8 us (0.909)
  local copies, waits for them, and re-layouts: 6.1 us -> 0 us
  Pallas kernels: 48.2 us -> 49.3 us
    unnamed x10 -> x0, local copies, waits for them, and re-layouts: 6.1 us -> none
    pallas_call x0 -> x1, Pallas kernels: none -> 2.48 us  [shards(): pl.pallas_call(finish, out_shape=(jax.ShapeDtypeStruct((TOK, D), BF16), j...]
    pallas_call x1, Pallas kernels: 48.2 us -> 46.8 us  [shards(): pl.pallas_call(kernel, out_shape=(jax.ShapeDtypeStruct((TOK, D), BF16), j...]
where the time goes in v3:
time: 50.8 us; the launch traced here: 50.6 us
  Pallas kernels  49.3 us (97%)
  between operations  1.29 us (3%)
    pallas_call x1, Pallas kernels, shards(): pl.pallas_call(kernel, out_shape=(jax.ShapeDtypeStruct((TOK, D), BF16), j...  46.8 us
    pallas_call x1, Pallas kernels, shards(): pl.pallas_call(finish, out_shape=(jax.ShapeDtypeStruct((TOK, D), BF16), j...  2.48 us

profile of v3, /device:TPU:1, one launch (start us, length us, event | category | flops | bytes accessed | tf_op | source)
XLA Modules:
  0.0 50.6 jit_solution(14527657873665669536)
XLA Ops:
  1.3 46.8 %shard_map.68 = (bf16[512,2048]{1,0:T(8,128)(2,1)}, f32[64,512]{1,0:T(8,128)}) custom-call(bf16[512,2048]{1,0:T(8,128)(2,1)} %bitcast.7, bf16[512,512]{1,0:T(8,128)(2,1)} %bitcast.8, bf16[64,512]{1,0:T(8,128)(2,1)} %bitcast.9, s32[1,16]{1,0:T(1,128)} %len_ref.1, f32[1,1]{1,0:T(1,128)} %bitcast.6.thr_ref), custom_call_target="tpu_custom_call" | custom-call | tf_op jit(solution)/shard_map/pallas_call | solution.py:384
  48.1 2.5 %shard_map.69 = (bf16[512,2048]{1,0:T(8,128)(2,1)}, f32[64,512]{1,0:T(8,128)}) custom-call(bf16[512,2048]{1,0:T(8,128)(2,1)} %get-tuple-element.6.act_in, f32[64,512]{1,0:T(8,128)} %get-tuple-element.7.wg_in), custom_call_target="tpu_custom_call" | custom-call | tf_op jit(solution)/shard_map/pallas_call | solution.py:426

commit v4 on v3

--- a/solution.py
+++ b/solution.py
@@ -11,14 +11,14 @@
 D, KV, TOK, PAT = 2048, 512, 512, 16
 POS = {2: 0, 1: 1, 3: 2, 0: 3}
 GROUPS = ((0, 1), (1, 3), (3, 4))
-N_SEMS = 109
+N_SEMS = 112
 VMEM = 58000 * 1024
 
 
 def kernel(
     acts_hbm, kg_hbm, w_hbm, len_ref, thr_ref, act_out, wg_out,
     acts, kg, kgs, kgt, sct, wr, act_v,
-    zv, zr, z2s, z2r, z9s, z9r,
+    zv, zr, z9s, z9r,
     pb, pc, pf, ra, cb, rx, ss, ra2, cb2, rx2, wsw,
     ssem, rsem, wsem, lsem,
 ):
@@ -57,8 +57,8 @@
     load_w.start()
 
     near = [dev(dc=1), dev(dx=1), dev(dx=-1), dev(dy=1), dev(dy=-1)]
-    zs = [1, -1, 2, -2, 3, -3, 4, -4]
-    partners = near + [dev(dz=k) for k in zs] + [dev(dz=4, dc=1), dev(dz=-4, dc=1)]
+    zs = [8] + [s * k for k in range(7, 0, -1) for s in (1, -1)]
+    partners = near + [dev(dz=k) for k in zs]
     barrier = pltpu.get_barrier_semaphore()
     for who in partners:
         pl.semaphore_signal(barrier, inc=1, device_id=who, device_id_type=MESH)
@@ -163,45 +163,19 @@
     share_kg.wait_recv()
     kgt[:, 512:1024] = kgs[...].T
 
-    for c in z1[0::2]:
+
+    for c in z1:
         c.wait_recv()
-    up = zr[0] + zr[2] + zr[4] + zr[6]
-    z2s[0] = up
-    z2 = [
-        send(z2s.at[0], z2r.at[0, 0], dev(dz=4)),
-        send(z2s.at[0], z2r.at[1, 0], dev(dz=4, dc=1)),
-    ]
-    for c in z1[1::2]:
-        c.wait_recv()
-    down = zr[1] + zr[3] + zr[5]
-    z2s[1] = down
-    z2 += [
-        send(z2s.at[1], z2r.at[0, 1], dev(dz=-4)),
-        send(z2s.at[1], z2r.at[1, 1], dev(dz=-4, dc=1)),
-    ]
-    nine = zv[...] + up + (down + zr[7])
-    z9s[...] = nine
-    z2.append(send(z9s, z9r, dev(dc=1)))
-
-    for d1 in (1, 3):
-        for h in range(2):
-            second_forward(h, d1)
-    for h in range(2):
-        second_forward(h, 2)
-
-    load_w.wait()
-    for h in range(2):
-        for d1 in range(4):
-            for c in g_b2[h, d1]:
-                c.wait_recv()
-    share_w = [
-        send(wr.at[dy, :, core], wr.at[dy, :, core], dev(dc=1)) for dy in range(4)
-    ]
-
-    for c in z2:
-        c.wait_recv()
+    both = zv[...]
+    for i in range(15):
+        both = both + zr[i]
+    z9s[...] = both
+    give = send(z9s, z9r, dev(dc=1))
     thr = thr_ref[0, 0]
-    for s, total in ((0, nine + (z2r[0, 0] + z2r[0, 1])), (1, z9r[...] + (z2r[1, 0] + z2r[1, 1]))):
+    for s in range(2):
+        if s == 1:
+            give.wait_recv()
+        total = z9r[...] if s else both
         factor = thr / jnp.maximum(jnp.sqrt(total), thr)
         cols = slice(512 * s, 512 * s + 512)
         sct[:, cols] = (kgt[:, cols].astype(F32) * factor).astype(BF16)
@@ -278,33 +252,6 @@
             for p in range(lo, hi):
                 ss[h, p] = (pf[h, p] + rx[h, 0, p].astype(F32) + rx[h, 1, p].astype(F32)).T
 
-    product(((2, 2), (2, 1)))
-    product(((2, 3), (1, 2)))
-    send_a(0)
-    product(((3, 2), (1, 1)))
-    send_b(0)
-    send_a(1)
-    product(((1, 3), (3, 1)))
-    product(((3, 3), (0, 2)))
-    send_b(1)
-    product(((2, 0), (0, 1)))
-    send_a(2)
-    product(((0, 3), (1, 0)))
-    product(((3, 0), (0, 0)))
-    send_b(2)
-    send_c(0)
-
-    send_c(1)
-    gathered(0)
-    p2a = [
-        (
-            send(ss.at[h, 0, pl.ds(0, 64)], ra2.at[h, 0], step[1 - h](1)),
-            send(ss.at[h, 0, pl.ds(64, 64)], ra2.at[h, 1], step[1 - h](-1)),
-        )
-        for h in range(2)
-    ]
-    send_c(2)
-
     def act_rows(dy):
         share_w[dy].wait_recv()
         for dx in (0, 2):
@@ -313,8 +260,45 @@
             act_v[:, columns(dy, dx)] = out[:, :128]
             act_v[:, columns(dy, dx + 1)] = out[:, 128:]
 
+    product(((2, 2), (2, 1)))
+    product(((2, 3), (1, 2)))
+    send_a(0)
+    product(((3, 2), (1, 1)))
+    send_b(0)
+    send_a(1)
+    for d1 in (1, 3):
+        for h in range(2):
+            second_forward(h, d1)
+    product(((1, 3), (3, 1)))
+    product(((3, 3), (0, 2)))
+    send_c(0)
+    send_b(1)
+    for h in range(2):
+        second_forward(h, 2)
+    product(((2, 0), (0, 1)))
+    product(((0, 3), (1, 0)))
+    send_a(2)
+    product(((3, 0), (0, 0)))
+    send_c(1)
+    send_b(2)
+    gathered(0)
+    p2a = [
+        (
+            send(ss.at[h, 0, pl.ds(0, 64)], ra2.at[h, 0], step[1 - h](1)),
+            send(ss.at[h, 0, pl.ds(64, 64)], ra2.at[h, 1], step[1 - h](-1)),
+        )
+        for h in range(2)
+    ]
+    load_w.wait()
+    for h in range(2):
+        for d1 in range(4):
+            for c in g_b2[h, d1]:
+                c.wait_recv()
+    share_w = [
+        send(wr.at[dy, :, core], wr.at[dy, :, core], dev(dc=1)) for dy in range(4)
+    ]
+
     act_rows(0)
-    act_rows(1)
 
     gathered(1)
     def last(src, h, s, c):
@@ -329,6 +313,8 @@
             cb2[h, s] = ss[h, 1 + s, 64 * s : 64 * s + 64] + ra2[h, s]
             last(cb2.at[h, s], h, s, s)
 
+    send_c(2)
+    act_rows(1)
     act_rows(2)
     act_rows(3)
     store = pltpu.make_async_copy(act_v, act_out, lsem.at[4])
@@ -398,9 +384,7 @@
             v((4, 4, 2, 64, KV), BF16),
             v((TOK, D), BF16),
             v((1, TOK), F32),
-            v((8, 1, TOK), F32),
-            v((2, 1, TOK), F32),
-            v((2, 2, 1, TOK), F32),
+            v((15, 1, TOK), F32),
             v((1, TOK), F32),
             v((1, TOK), F32),
             v((2, 3, 4, 128, 128), BF16),

time: 50.8 us -> 49.6 us (0.976)
  Pallas kernels: 49.3 us -> 48.1 us
    pallas_call x1, Pallas kernels: 46.8 us -> 45.6 us  [shards(): pl.pallas_call(kernel, out_shape=(jax.ShapeDtypeStruct((TOK, D), BF16), j...]
where the time goes in v4:
time: 49.6 us; the launch traced here: 49.4 us
  Pallas kernels  48.1 us (97%)
  between operations  1.29 us (3%)
    pallas_call x1, Pallas kernels, shards(): pl.pallas_call(kernel, out_shape=(jax.ShapeDtypeStruct((TOK, D), BF16), j...  45.6 us
    pallas_call x1, Pallas kernels, shards(): pl.pallas_call(finish, out_shape=(jax.ShapeDtypeStruct((TOK, D), BF16), j...  2.48 us

profile of v4, /device:TPU:1, one launch (start us, length us, event | category | flops | bytes accessed | tf_op | source)
XLA Modules:
  0.0 49.4 jit_solution(14106093436364505499)
XLA Ops:
  1.3 45.6 %shard_map.68 = (bf16[512,2048]{1,0:T(8,128)(2,1)}, f32[64,512]{1,0:T(8,128)}) custom-call(bf16[512,2048]{1,0:T(8,128)(2,1)} %bitcast.7, bf16[512,512]{1,0:T(8,128)(2,1)} %bitcast.8, bf16[64,512]{1,0:T(8,128)(2,1)} %bitcast.9, s32[1,16]{1,0:T(1,128)} %len_ref.1, f32[1,1]{1,0:T(1,128)} %bitcast.6.thr_ref), custom_call_target="tpu_custom_call" | custom-call | tf_op jit(solution)/shard_map/pallas_call | solution.py:370
  46.9 2.5 %shard_map.69 = (bf16[512,2048]{1,0:T(8,128)(2,1)}, f32[64,512]{1,0:T(8,128)}) custom-call(bf16[512,2048]{1,0:T(8,128)(2,1)} %get-tuple-element.6.act_in, f32[64,512]{1,0:T(8,128)} %get-tuple-element.7.wg_in), custom_call_target="tpu_custom_call" | custom-call | tf_op jit(solution)/shard_map/pallas_call | solution.py:410

commit v5 on v4

--- a/solution.py
+++ b/solution.py
@@ -58,7 +58,7 @@
 
     near = [dev(dc=1), dev(dx=1), dev(dx=-1), dev(dy=1), dev(dy=-1)]
     zs = [8] + [s * k for k in range(7, 0, -1) for s in (1, -1)]
-    partners = near + [dev(dz=k) for k in zs]
+    partners = [dev(dz=k) for k in zs] + near
     barrier = pltpu.get_barrier_semaphore()
     for who in partners:
         pl.semaphore_signal(barrier, inc=1, device_id=who, device_id_type=MESH)
@@ -154,11 +154,6 @@
     for h in range(2):
         for d1 in (1, 3):
             g_b1[h, d1] = second(h, d1)
-    for h in range(2):
-        for c in g_a2[h]:
-            c.wait_recv()
-        g_b1[h, 2] = second(h, 2)
-        second_forward(h, 0)
 
     share_kg.wait_recv()
     kgt[:, 512:1024] = kgs[...].T
@@ -266,6 +261,11 @@
     product(((3, 2), (1, 1)))
     send_b(0)
     send_a(1)
+    for h in range(2):
+        for c in g_a2[h]:
+            c.wait_recv()
+        g_b1[h, 2] = second(h, 2)
+        second_forward(h, 0)
     for d1 in (1, 3):
         for h in range(2):
             second_forward(h, d1)

time: 49.6 us -> 48.2 us (0.972)
  Pallas kernels: 48.1 us -> 46.7 us
    pallas_call x1, Pallas kernels: 45.6 us -> 44.2 us  [shards(): pl.pallas_call(kernel, out_shape=(jax.ShapeDtypeStruct((TOK, D), BF16), j...]
where the time goes in v5:
time: 48.2 us; the launch traced here: 48 us
  Pallas kernels  46.7 us (97%)
  between operations  1.29 us (3%)
    pallas_call x1, Pallas kernels, shards(): pl.pallas_call(kernel, out_shape=(jax.ShapeDtypeStruct((TOK, D), BF16), j...  44.2 us
    pallas_call x1, Pallas kernels, shards(): pl.pallas_call(finish, out_shape=(jax.ShapeDtypeStruct((TOK, D), BF16), j...  2.48 us

profile of v5, /device:TPU:1, one launch (start us, length us, event | category | flops | bytes accessed | tf_op | source)
XLA Modules:
  0.0 48.0 jit_solution(9510389319782247987)
XLA Ops:
  1.3 44.2 %shard_map.68 = (bf16[512,2048]{1,0:T(8,128)(2,1)}, f32[64,512]{1,0:T(8,128)}) custom-call(bf16[512,2048]{1,0:T(8,128)(2,1)} %bitcast.7, bf16[512,512]{1,0:T(8,128)(2,1)} %bitcast.8, bf16[64,512]{1,0:T(8,128)(2,1)} %bitcast.9, s32[1,16]{1,0:T(1,128)} %len_ref.1, f32[1,1]{1,0:T(1,128)} %bitcast.6.thr_ref), custom_call_target="tpu_custom_call" | custom-call | tf_op jit(solution)/shard_map/pallas_call | solution.py:370
  45.5 2.5 %shard_map.69 = (bf16[512,2048]{1,0:T(8,128)(2,1)}, f32[64,512]{1,0:T(8,128)}) custom-call(bf16[512,2048]{1,0:T(8,128)(2,1)} %get-tuple-element.6.act_in, f32[64,512]{1,0:T(8,128)} %get-tuple-element.7.wg_in), custom_call_target="tpu_custom_call" | custom-call | tf_op jit(solution)/shard_map/pallas_call | solution.py:410
